TPU v7x, 32 devices: a whole 2x2x4 slice. The times are simulated.
32 devices in a mesh: span: 2 (over y), tmpl: 2 (over x), stn: 8 (over z, core).
Axes of the slice: x: 2, y: 2, z: 4, core: 2. Of those that a mesh axis runs over, the one named last changes fastest.
Arguments:
- signal: bfloat16 [3072, 8192], P('stn', ('span', 'tmpl')), parts along dimension 1, may hold values from -110 to 110
- waveforms: bfloat16 [16, 4, 8, 300], P('tmpl'), may hold values from -40 to 40
- station_groups: int32 [16, 4], P('tmpl'), may hold values from 0 to 7, all different within a row; in each aligned block of 8 rows (0 to 7, 8 to 15, ...) at most 8 rows name the same one
- channel_offsets: int32 [16, 4, 8], P('tmpl'), may hold values from 0 to 383
- moveouts: int32 [16, 4, 8], P('tmpl'), may hold values from 0 to 639
Outputs:
- stack: float32 [16, 6144], P(('tmpl', 'stn'), 'span'), parts along dimension 1
There are 2 independent parts, one for each index of `span`. A program takes and returns all parts, laid end to end along the dimension named above; an argument that names none is the same for every part. Nothing has to cross between parts.
Inputs may be any that keep to these rules, and one draw needn't show every extreme that they name: `station_groups`: A template's 4 station groups are distinct. Among the 8 templates of one index of tmpl, at most 8 touch any one station group, and in every draw some station group is touched by exactly 8 of them.
All inputs are finite; a program needn't handle non-finite values.
Results may differ from a plain program's by a relative error of at most 0.0003.
Values may be sent and summed in bfloat16 or wider, within the bound.
A program may use at most 64 MiB of HBM per device.

v0:
```python
import functools

import jax
import jax.numpy as jnp
from jax import lax
from jax.experimental import pallas as pl
from jax.experimental.pallas import tpu as pltpu
from jax.sharding import PartitionSpec as P

NT = 3072
EPS = 1e-05
LANES = 128
ROWS = 16
MESH = pl.DeviceIdType.MESH
F32 = jnp.float32
BF16 = jnp.bfloat16


def iota(shape, axis):
    return lax.broadcasted_iota(jnp.int32, shape, axis)


def kernel(
    n_t, n_s, sg_hbm, off_hbm, mov_hbm, wave_hbm, sig_hbm, out_ref,
    sg_ref, off_ref, mov_ref, wave_ref, pick, sig, asked, wanted, reply, landed, rows, toep, band, winv, wrev, stacks, parts,
    load_sem, ask_send, ask_recv, row_send, row_recv, part_send, part_recv,
):
    me_t = lax.axis_index("tmpl")
    me_s = lax.axis_index("stn")
    touch, n_k = sg_ref.shape
    n_slot = off_ref.shape[2]
    length = wave_ref.shape[3]
    chans, span = sig.shape
    slots = n_k * n_slot
    span_blocks = span // LANES
    all_blocks = span_blocks * n_t
    n_circ = -(-length // LANES)
    n_band = n_circ + 1
    out_blocks = NT // LANES
    chunks = slots // ROWS
    per_chunk = ROWS // n_slot
    own = n_k // n_s

    barrier = pltpu.get_barrier_semaphore()
    for d in range(1, n_t):
        pl.semaphore_signal(
            barrier, inc=1, device_id={"tmpl": lax.rem(me_t + d, n_t)}, device_id_type=MESH
        )
    for d in range(1, n_s):
        pl.semaphore_signal(
            barrier, inc=1, device_id={"stn": lax.rem(me_s + d, n_s)}, device_id_type=MESH
        )

    operands = (
        (sg_hbm, sg_ref), (off_hbm, off_ref), (sig_hbm, sig), (wave_hbm, wave_ref), (mov_hbm, mov_ref)
    )
    loads = [
        pltpu.make_async_copy(a, b, load_sem.at[i]) for i, (a, b) in enumerate(operands)
    ]
    for load in loads:
        load.start()

    gap = iota((n_band * LANES, LANES), 0) - iota((n_band * LANES, LANES), 1)
    band[...] = jnp.logical_and(gap >= 0, gap < length).astype(F32).astype(BF16)
    turn = jnp.bitwise_and(iota((LANES, LANES), 0) + iota((LANES, LANES), 1), LANES - 1)
    flip = (turn == 0).astype(F32).astype(BF16)

    loads[0].wait()
    loads[1].wait()

    sub = iota((n_slot, LANES), 0)
    for k in range(n_k):
        at = jnp.int32(0)
        for g in range(1, touch):
            at = jnp.where(sg_ref[g, k] == me_s, g, at)
        pick[k] = at
        tile = jnp.zeros((n_slot, LANES), jnp.int32)
        for s in range(n_slot):
            tile = jnp.where(sub == s, off_ref[k, at, s], tile)
        asked[k * n_slot : (k + 1) * n_slot, :] = tile

    pl.semaphore_wait(barrier, n_t - 1 + n_s - 1)

    def ask(d):
        return pltpu.make_async_remote_copy(
            src_ref=asked,
            dst_ref=wanted.at[d - 1],
            send_sem=ask_send.at[d - 1],
            recv_sem=ask_recv.at[d - 1],
            device_id={"tmpl": lax.rem(me_t + d, n_t)},
            device_id_type=MESH,
        )

    def send_rows(d, i):
        part = pl.ds(pl.multiple_of(i * ROWS, ROWS), ROWS)
        return pltpu.make_async_remote_copy(
            src_ref=reply.at[d - 1, part],
            dst_ref=landed.at[d - 1, part],
            send_sem=row_send.at[d - 1, i],
            recv_sem=row_recv.at[d - 1, i],
            device_id={"tmpl": lax.rem(me_t + n_t - d, n_t)},
            device_id_type=MESH,
        )

    for d in range(1, n_t):
        ask(d).start()

    piece = min(span, 512)

    def one_hot(ref):
        return (iota((slots, chans), 1) == ref[:, 0:1]).astype(F32).astype(BF16)

    def place(tile, source, first):
        count = tile.shape[0]
        for j in range(tile.shape[1] // LANES):
            start = first * all_blocks + source * span_blocks + j
            rows[pl.ds(start, count, stride=all_blocks), :] = tile[:, j * LANES : (j + 1) * LANES]

    loads[2].wait()
    mine = one_hot(asked)
    for c in range(span // piece):
        got = jnp.dot(mine, sig[:, c * piece : (c + 1) * piece], preferred_element_type=F32)
        for j in range(piece // LANES):
            start = me_t * span_blocks + c * (piece // LANES) + j
            rows[pl.ds(start, slots, stride=all_blocks), :] = got[:, j * LANES : (j + 1) * LANES]

    loads[3].wait()
    waves = []
    for k in range(n_k):
        live = sg_ref[0, k] == me_s
        for g in range(1, touch):
            live = jnp.logical_or(live, sg_ref[g, k] == me_s)
        wave = wave_ref[k, pick[k]].astype(F32)
        waves.append(jnp.where(live, wave, 0.0))
    waves = jnp.concatenate(waves, axis=0)
    power = jnp.sum(waves * waves, axis=1, keepdims=True) / length
    scale = lax.rsqrt(power + EPS) / length
    winv[...] = jnp.broadcast_to(scale, winv.shape)
    for j in range(n_circ):
        count = min(LANES, length - j * LANES)
        wrev[:, j * LANES : (j + 1) * LANES] = jnp.dot(
            waves[:, j * LANES : j * LANES + count].astype(BF16),
            flip[:count],
            preferred_element_type=F32,
        )

    for d in range(1, n_t):
        ask(d).wait_recv()
        theirs = one_hot(wanted.at[d - 1])
        for c in range(span // piece):
            cut = slice(c * piece, (c + 1) * piece)
            reply[d - 1, :, cut] = jnp.dot(
                theirs, sig[:, cut], preferred_element_type=F32
            ).astype(BF16)
        for i in range(chunks):
            send_rows(d, i).start()

    lower = (iota((LANES, LANES), 0) >= iota((LANES, LANES), 1)).astype(F32).astype(BF16) > 0

    def circle(line):
        first = pltpu.roll(jnp.broadcast_to(line, (ROWS, LANES)), 0, 1, stride=1, stride_axis=0)
        first = first.astype(BF16)
        return jnp.concatenate(
            [first] + [pltpu.roll(first, r, 1) for r in range(ROWS, LANES, ROWS)], axis=0
        )

    def build(k, carry):
        tile = wrev[pl.ds(pl.multiple_of(k * n_slot, n_slot), n_slot), :]
        zero = jnp.zeros((LANES, LANES), BF16)
        for s in range(n_slot):
            before = zero
            for j in range(n_band):
                here = zero
                if j < n_circ:
                    here = circle(tile[s : s + 1, j * LANES : (j + 1) * LANES])
                toep[k * n_slot + s, j * LANES : (j + 1) * LANES, :] = jnp.where(
                    lower, here, before
                )
                before = here
        return carry

    lax.fori_loop(0, n_k, build, 0)

    def send_part(k):
        return pltpu.make_async_remote_copy(
            src_ref=stacks.at[k],
            dst_ref=parts.at[me_s, lax.rem(k, own)],
            send_sem=part_send.at[k],
            recv_sem=part_recv.at[me_s, lax.rem(k, own)],
            device_id={"stn": k // own},
            device_id_type=MESH,
        )

    lane = iota((out_blocks, LANES), 1)
    loads[4].wait()

    def template(k, carry):
        at = pick[k]
        segs = []
        prods = []
        for s in range(n_slot):
            move = mov_ref[k, at, s]
            blocks = move // LANES
            rest = move - blocks * LANES
            turn = lax.rem(LANES - rest, LANES)
            base = (k * n_slot + s) * all_blocks + blocks
            turned = [
                pltpu.roll(rows[pl.ds(base + j, out_blocks), :], turn, 1) for j in range(n_band + 1)
            ]
            keep = lane < LANES - rest
            seg = jnp.concatenate(
                [jnp.where(keep, turned[j], turned[j + 1]) for j in range(n_band)], axis=1
            )
            segs.append(seg)
            prods.append(
                jnp.dot(seg.astype(BF16), toep[k * n_slot + s], preferred_element_type=F32)
            )
        seg = jnp.concatenate(segs, axis=0)
        square = seg * seg
        high = square.astype(BF16)
        low = (square - high.astype(F32)).astype(BF16)
        bands = band[...]
        energy = jnp.dot(high, bands, preferred_element_type=F32)
        energy = energy + jnp.dot(low, bands, preferred_element_type=F32)
        inverse = lax.rsqrt(energy / length + EPS)
        scales = winv[pl.ds(pl.multiple_of(k * n_slot, n_slot), n_slot), :]
        total = jnp.zeros((out_blocks, LANES), F32)
        for s in range(n_slot):
            part = inverse[s * out_blocks : (s + 1) * out_blocks]
            total = total + prods[s] * (part * scales[s : s + 1, :])
        stacks[k] = total

        @pl.when(k // own != me_s)
        def _():
            send_part(k).start()

        return carry

    def chunk(i, carry):
        for d in range(1, n_t):
            send_rows(d, i).wait_recv()
            tile = landed[d - 1, pl.ds(pl.multiple_of(i * ROWS, ROWS), ROWS), :].astype(F32)
            place(tile, lax.rem(me_t + d, n_t), i * ROWS)
        return lax.fori_loop(i * per_chunk, (i + 1) * per_chunk, template, carry)

    lax.fori_loop(0, chunks, chunk, 0)

    for d in range(1, n_t):
        ask(d).wait_send()
        for i in range(chunks):
            send_rows(d, i).wait_send()

    for r in range(own):
        out_ref[r] = stacks[me_s * own + r]
    for d in range(1, n_s):
        other = lax.rem(me_s + d, n_s)
        for r in range(own):
            pltpu.make_async_remote_copy(
                src_ref=stacks.at[0],
                dst_ref=parts.at[other, r],
                send_sem=part_send.at[0],
                recv_sem=part_recv.at[other, r],
                device_id={"stn": other},
                device_id_type=MESH,
            ).wait_recv()
            out_ref[r] = out_ref[r] + parts[other, r]
    for d in range(1, n_s):
        other = lax.rem(me_s + d, n_s)
        for r in range(own):
            send_part(other * own + r).wait_send()


def shards(signal, waveforms, station_groups, channel_offsets, moveouts):
    n_t = lax.axis_size("tmpl")
    n_s = lax.axis_size("stn")
    n_k, touch, n_slot, length = waveforms.shape
    chans, span = signal.shape
    slots = n_k * n_slot
    out_blocks = NT // LANES
    n_circ = -(-length // LANES)
    chunks = slots // ROWS
    own = n_k // n_s
    dma = pltpu.SemaphoreType.DMA
    stack = pl.pallas_call(
        functools.partial(kernel, n_t, n_s),
        out_shape=jax.ShapeDtypeStruct((own, out_blocks, LANES), F32),
        in_specs=[pl.BlockSpec(memory_space=pl.ANY)] * 5,
        out_specs=pl.BlockSpec(memory_space=pltpu.VMEM),
        scratch_shapes=[
            pltpu.SMEM((touch, n_k), jnp.int32),
            pltpu.SMEM((n_k, touch, n_slot), jnp.int32),
            pltpu.SMEM((n_k, touch, n_slot), jnp.int32),
            pltpu.VMEM((n_k, touch, n_slot, length), BF16),
            pltpu.SMEM((n_k,), jnp.int32),
            pltpu.VMEM((chans, span), BF16),
            pltpu.VMEM((slots, LANES), jnp.int32),
            pltpu.VMEM((n_t - 1, slots, LANES), jnp.int32),
            pltpu.VMEM((n_t - 1, slots, span), BF16),
            pltpu.VMEM((n_t - 1, slots, span), BF16),
            pltpu.VMEM((slots * n_t * span // LANES, LANES), F32),
            pltpu.VMEM((slots, (n_circ + 1) * LANES, LANES), BF16),
            pltpu.VMEM(((n_circ + 1) * LANES, LANES), BF16),
            pltpu.VMEM((slots, LANES), F32),
            pltpu.VMEM((slots, n_circ * LANES), F32),
            pltpu.VMEM((n_k, out_blocks, LANES), F32),
            pltpu.VMEM((n_s, own, out_blocks, LANES), F32),
            dma((5,)),
            dma((n_t - 1,)),
            dma((n_t - 1,)),
            dma((n_t - 1, chunks)),
            dma((n_t - 1, chunks)),
            dma((n_k,)),
            dma((n_s, own)),
        ],
        compiler_params=pltpu.CompilerParams(
            collective_id=0, has_side_effects=True, vmem_limit_bytes=63 * 1024 * 1024
        ),
    )(station_groups.T, channel_offsets, moveouts, waveforms, signal)
    return stack.reshape(own, NT)


def solution(mesh):
    in_specs = (
        P("stn", ("span", "tmpl")),
        P("tmpl", None, None, None),
        P("tmpl", None),
        P("tmpl", None, None),
        P("tmpl", None, None),
    )
    out_specs = P(("tmpl", "stn"), "span")
    return jax.shard_map(shards, mesh=mesh, in_specs=in_specs, out_specs=out_specs, check_vma=False)
```

profile of v0, /device:TPU:0, one launch (start us, length us, event | category | flops | bytes accessed | tf_op | source)
XLA Modules:
  0.0 21.9 jit_solution(14792142477641940082)
XLA Ops:
  0.0 20.6 %shard_map.55 = f32[1,24,128]{2,1,0:T(8,128)} custom-call(s32[4,8]{1,0:T(4,128)} %bitcast.3, s32[8,4,8]{2,1,0:T(4,128)} %off_hbm.1, s32[8,4,8]{2,1,0:T(4,128)} %mov_hbm.1, bf16[8,4,8,300]{3,2,1,0:T(8,128)(2,1)} %wave_hbm.1, bf16[384,2048]{1,0:T(8,128)(2,1)} %sig_hbm.1), custom_call_target="tpu_custom_call" | custom-call | tf_op jit(solution)/shard_map/pallas_call | solution.py:284
  20.6 1.3 %copy.7 = f32[1,3072]{1,0:T(1,128)} copy(f32[1,3072]{1,0:T(1,128)} %bitcast.2) | data formatting | bytes 24576
where the time goes:
time: 22.2 us; the launch traced here: 21.9 us
  Pallas kernels  20.6 us (93%)
  local copies, waits for them, and re-layouts  1.31 us (6%)
    pallas_call x1, Pallas kernels, shards(): pl.pallas_call(functools.partial(kernel, n_t, n_s), out_shape=jax.ShapeDt...  20.6 us
    unnamed x1, local copies, waits for them, and re-layouts  1.31 us

commit v1 on v0

--- a/solution.py
+++ b/solution.py
@@ -68,16 +68,19 @@
     loads[0].wait()
     loads[1].wait()
 
+    lane = iota((n_slot, LANES), 1)
     sub = iota((n_slot, LANES), 0)
+    tile = jnp.zeros((n_slot, LANES), jnp.int32)
     for k in range(n_k):
         at = jnp.int32(0)
         for g in range(1, touch):
             at = jnp.where(sg_ref[g, k] == me_s, g, at)
         pick[k] = at
-        tile = jnp.zeros((n_slot, LANES), jnp.int32)
+        column = jnp.zeros((n_slot, LANES), jnp.int32)
         for s in range(n_slot):
-            tile = jnp.where(sub == s, off_ref[k, at, s], tile)
-        asked[k * n_slot : (k + 1) * n_slot, :] = tile
+            column = jnp.where(sub == s, off_ref[k, at, s], column)
+        tile = jnp.where(lane == k, column, tile)
+    asked[...] = tile
 
     pl.semaphore_wait(barrier, n_t - 1 + n_s - 1)
 
@@ -107,8 +110,16 @@
 
     piece = min(span, 512)
 
-    def one_hot(ref):
-        return (iota((slots, chans), 1) == ref[:, 0:1]).astype(F32).astype(BF16)
+    def one_hot(tile):
+        number = iota((n_slot, chans), 1)
+        picked = [
+            (number == jnp.broadcast_to(tile[:, k : k + 1], (n_slot, chans))).astype(F32)
+            for k in range(n_k)
+        ]
+        return jnp.concatenate(picked, axis=0).astype(BF16)
+
+    def order(i):
+        return lax.rem(me_s * own // per_chunk + 1 + i, chunks)
 
     def place(tile, source, first):
         count = tile.shape[0]
@@ -117,12 +128,23 @@
             rows[pl.ds(start, count, stride=all_blocks), :] = tile[:, j * LANES : (j + 1) * LANES]
 
     loads[2].wait()
-    mine = one_hot(asked)
+    mine = one_hot(tile)
     for c in range(span // piece):
         got = jnp.dot(mine, sig[:, c * piece : (c + 1) * piece], preferred_element_type=F32)
         for j in range(piece // LANES):
             start = me_t * span_blocks + c * (piece // LANES) + j
             rows[pl.ds(start, slots, stride=all_blocks), :] = got[:, j * LANES : (j + 1) * LANES]
+
+    for d in range(1, n_t):
+        ask(d).wait_recv()
+        theirs = one_hot(wanted[d - 1])
+        for c in range(span // piece):
+            cut = slice(c * piece, (c + 1) * piece)
+            reply[d - 1, :, cut] = jnp.dot(
+                theirs, sig[:, cut], preferred_element_type=F32
+            ).astype(BF16)
+        for i in range(chunks):
+            send_rows(d, order(i)).start()
 
     loads[3].wait()
     waves = []
@@ -144,17 +166,6 @@
             preferred_element_type=F32,
         )
 
-    for d in range(1, n_t):
-        ask(d).wait_recv()
-        theirs = one_hot(wanted.at[d - 1])
-        for c in range(span // piece):
-            cut = slice(c * piece, (c + 1) * piece)
-            reply[d - 1, :, cut] = jnp.dot(
-                theirs, sig[:, cut], preferred_element_type=F32
-            ).astype(BF16)
-        for i in range(chunks):
-            send_rows(d, i).start()
-
     lower = (iota((LANES, LANES), 0) >= iota((LANES, LANES), 1)).astype(F32).astype(BF16) > 0
 
     def circle(line):
@@ -191,10 +202,10 @@
             device_id_type=MESH,
         )
 
-    lane = iota((out_blocks, LANES), 1)
+    spot = iota((out_blocks, LANES), 1)
     loads[4].wait()
 
-    def template(k, carry):
+    def template(k):
         at = pick[k]
         segs = []
         prods = []
@@ -207,7 +218,7 @@
             turned = [
                 pltpu.roll(rows[pl.ds(base + j, out_blocks), :], turn, 1) for j in range(n_band + 1)
             ]
-            keep = lane < LANES - rest
+            keep = spot < LANES - rest
             seg = jnp.concatenate(
                 [jnp.where(keep, turned[j], turned[j + 1]) for j in range(n_band)], axis=1
             )
@@ -228,20 +239,27 @@
         for s in range(n_slot):
             part = inverse[s * out_blocks : (s + 1) * out_blocks]
             total = total + prods[s] * (part * scales[s : s + 1, :])
-        stacks[k] = total
-
-        @pl.when(k // own != me_s)
-        def _():
-            send_part(k).start()
-
-        return carry
-
-    def chunk(i, carry):
+        return total
+
+    def chunk(step, carry):
+        i = order(step)
         for d in range(1, n_t):
             send_rows(d, i).wait_recv()
             tile = landed[d - 1, pl.ds(pl.multiple_of(i * ROWS, ROWS), ROWS), :].astype(F32)
             place(tile, lax.rem(me_t + d, n_t), i * ROWS)
-        return lax.fori_loop(i * per_chunk, (i + 1) * per_chunk, template, carry)
+        names = [
+            i * per_chunk + lax.rem(me_s * own + 1 + q, per_chunk) for q in range(per_chunk)
+        ]
+        totals = [template(k) for k in names]
+        for k, total in zip(names, totals):
+            stacks[k] = total
+        for k in names:
+
+            @pl.when(k // own != me_s)
+            def _(k=k):
+                send_part(k).start()
+
+        return carry
 
     lax.fori_loop(0, chunks, chunk, 0)
 
@@ -293,8 +311,8 @@
             pltpu.VMEM((n_k, touch, n_slot, length), BF16),
             pltpu.SMEM((n_k,), jnp.int32),
             pltpu.VMEM((chans, span), BF16),
-            pltpu.VMEM((slots, LANES), jnp.int32),
-            pltpu.VMEM((n_t - 1, slots, LANES), jnp.int32),
+            pltpu.VMEM((n_slot, LANES), jnp.int32),
+            pltpu.VMEM((n_t - 1, n_slot, LANES), jnp.int32),
             pltpu.VMEM((n_t - 1, slots, span), BF16),
             pltpu.VMEM((n_t - 1, slots, span), BF16),
             pltpu.VMEM((slots * n_t * span // LANES, LANES), F32),

time: 22.2 us -> 21.3 us (0.959)
  Pallas kernels: 20.6 us -> 19.7 us
    pallas_call x1, Pallas kernels: 20.6 us -> 19.7 us  [shards(): pl.pallas_call(functools.partial(kernel, n_t, n_s), out_shape=jax.ShapeDt...]
where the time goes in v1:
time: 21.3 us; the launch traced here: 21.1 us
  Pallas kernels  19.7 us (92%)
  local copies, waits for them, and re-layouts  1.31 us (6%)
    pallas_call x1, Pallas kernels, shards(): pl.pallas_call(functools.partial(kernel, n_t, n_s), out_shape=jax.ShapeDt...  19.7 us
    unnamed x1, local copies, waits for them, and re-layouts  1.31 us

profile of v1, /device:TPU:0, one launch (start us, length us, event | category | flops | bytes accessed | tf_op | source)
XLA Modules:
  0.0 21.1 jit_solution(9056750118767706748)
XLA Ops:
  0.0 19.7 %shard_map.55 = f32[1,24,128]{2,1,0:T(8,128)} custom-call(s32[4,8]{1,0:T(4,128)} %bitcast.3, s32[8,4,8]{2,1,0:T(4,128)} %off_hbm.1, s32[8,4,8]{2,1,0:T(4,128)} %mov_hbm.1, bf16[8,4,8,300]{3,2,1,0:T(8,128)(2,1)} %wave_hbm.1, bf16[384,2048]{1,0:T(8,128)(2,1)} %sig_hbm.1), custom_call_target="tpu_custom_call" | custom-call | tf_op jit(solution)/shard_map/pallas_call | solution.py:302
  19.8 1.3 %copy.7 = f32[1,3072]{1,0:T(1,128)} copy(f32[1,3072]{1,0:T(1,128)} %bitcast.2) | data formatting | bytes 24576

commit v2 on v1

--- a/solution.py
+++ b/solution.py
@@ -38,6 +38,7 @@
     n_band = n_circ + 1
     out_blocks = NT // LANES
     chunks = slots // ROWS
+    ahead = chunks // 2
     per_chunk = ROWS // n_slot
     own = n_k // n_s
 
@@ -126,25 +127,6 @@
         for j in range(tile.shape[1] // LANES):
             start = first * all_blocks + source * span_blocks + j
             rows[pl.ds(start, count, stride=all_blocks), :] = tile[:, j * LANES : (j + 1) * LANES]
-
-    loads[2].wait()
-    mine = one_hot(tile)
-    for c in range(span // piece):
-        got = jnp.dot(mine, sig[:, c * piece : (c + 1) * piece], preferred_element_type=F32)
-        for j in range(piece // LANES):
-            start = me_t * span_blocks + c * (piece // LANES) + j
-            rows[pl.ds(start, slots, stride=all_blocks), :] = got[:, j * LANES : (j + 1) * LANES]
-
-    for d in range(1, n_t):
-        ask(d).wait_recv()
-        theirs = one_hot(wanted[d - 1])
-        for c in range(span // piece):
-            cut = slice(c * piece, (c + 1) * piece)
-            reply[d - 1, :, cut] = jnp.dot(
-                theirs, sig[:, cut], preferred_element_type=F32
-            ).astype(BF16)
-        for i in range(chunks):
-            send_rows(d, order(i)).start()
 
     loads[3].wait()
     waves = []
@@ -166,6 +148,25 @@
             preferred_element_type=F32,
         )
 
+    loads[2].wait()
+    for d in range(1, n_t):
+        ask(d).wait_recv()
+        theirs = one_hot(wanted[d - 1])
+        for c in range(span // piece):
+            cut = slice(c * piece, (c + 1) * piece)
+            reply[d - 1, :, cut] = jnp.dot(
+                theirs, sig[:, cut], preferred_element_type=F32
+            ).astype(BF16)
+        for i in range(ahead):
+            send_rows(d, order(i)).start()
+
+    mine = one_hot(tile)
+    for c in range(span // piece):
+        got = jnp.dot(mine, sig[:, c * piece : (c + 1) * piece], preferred_element_type=F32)
+        for j in range(piece // LANES):
+            start = me_t * span_blocks + c * (piece // LANES) + j
+            rows[pl.ds(start, slots, stride=all_blocks), :] = got[:, j * LANES : (j + 1) * LANES]
+
     lower = (iota((LANES, LANES), 0) >= iota((LANES, LANES), 1)).astype(F32).astype(BF16) > 0
 
     def circle(line):
@@ -191,6 +192,12 @@
         return carry
 
     lax.fori_loop(0, n_k, build, 0)
+
+    for d in range(1, n_t):
+        for i in range(ahead):
+            send_rows(d, order(i)).wait_send()
+        for i in range(ahead, chunks):
+            send_rows(d, order(i)).start()
 
     def send_part(k):
         return pltpu.make_async_remote_copy(
@@ -265,8 +272,8 @@
 
     for d in range(1, n_t):
         ask(d).wait_send()
-        for i in range(chunks):
-            send_rows(d, i).wait_send()
+        for i in range(ahead, chunks):
+            send_rows(d, order(i)).wait_send()
 
     for r in range(own):
         out_ref[r] = stacks[me_s * own + r]
@@ -331,7 +338,7 @@
             dma((n_s, own)),
         ],
         compiler_params=pltpu.CompilerParams(
-            collective_id=0, has_side_effects=True, vmem_limit_bytes=63 * 1024 * 1024
+            collective_id=0, has_side_effects=True, vmem_limit_bytes=55212 * 1024
         ),
     )(station_groups.T, channel_offsets, moveouts, waveforms, signal)
     return stack.reshape(own, NT)

time: 21.3 us -> 22.2 us (1.042)
  Pallas kernels: 19.7 us -> 20.6 us
    pallas_call x1, Pallas kernels: 19.7 us -> 20.6 us  [shards(): pl.pallas_call(functools.partial(kernel, n_t, n_s), out_shape=jax.ShapeDt...]
    unnamed x1 -> x3, local copies, waits for them, and re-layouts: 1.31 us -> 1.28 us
where the time goes in v2:
time: 22.2 us; the launch traced here: 21.9 us
  Pallas kernels  20.6 us (93%)
  local copies, waits for them, and re-layouts  1.28 us (6%)
    pallas_call x1, Pallas kernels, shards(): pl.pallas_call(functools.partial(kernel, n_t, n_s), out_shape=jax.ShapeDt...  20.6 us
    unnamed x3, local copies, waits for them, and re-layouts  1.28 us

profile of v2, /device:TPU:0, one launch (start us, length us, event | category | flops | bytes accessed | tf_op | source)
XLA Modules:
  0.0 21.9 jit_solution(18143103470535021743)
XLA Ops:
  0.0 0.0 copy-start
  0.0 0.7 %copy-done = s32[8,4]{0,1:T(4,128)S(1)} copy-done((s32[8,4]{0,1:T(4,128)S(1)}, s32[8,4]{0,1:T(4,128)}, u32[]{:S(2)}) %copy-start) | copy-done | bytes 152
  0.7 20.6 %shard_map.55 = f32[1,24,128]{2,1,0:T(8,128)S(1)} custom-call(s32[4,8]{1,0:T(4,128)S(1)} %bitcast.3, s32[8,4,8]{2,1,0:T(4,128)} %off_hbm.1, s32[8,4,8]{2,1,0:T(4,128)} %mov_hbm.1, bf16[8,4,8,300]{3,2,1,0:T(8,128)(2,1)} %wave_hbm.1, bf16[384,2048]{1,0:T(8,128)(2,1)} %sig_hbm.1), custom_call_target="tpu_custom_call" | custom-call | tf_op jit(solution)/shard_map/pallas_call | solution.py:309
  21.3 0.6 %copy.7 = f32[1,3072]{1,0:T(1,128)} copy(f32[1,3072]{1,0:T(1,128)S(1)} %bitcast.2) | data formatting | bytes 24576
Async XLA Ops:
  0.0 0.7 %copy-start = (s32[8,4]{0,1:T(4,128)S(1)}, s32[8,4]{0,1:T(4,128)}, u32[]{:S(2)}) copy-start(s32[8,4]{0,1:T(4,128)} %param.7) | copy-start | bytes 388

commit v3 on v1

--- a/solution.py
+++ b/solution.py
@@ -33,7 +33,7 @@
     chans, span = sig.shape
     slots = n_k * n_slot
     span_blocks = span // LANES
-    all_blocks = span_blocks * n_t
+    pitch = span_blocks * n_t + 1
     n_circ = -(-length // LANES)
     n_band = n_circ + 1
     out_blocks = NT // LANES
@@ -124,8 +124,8 @@
     def place(tile, source, first):
         count = tile.shape[0]
         for j in range(tile.shape[1] // LANES):
-            start = first * all_blocks + source * span_blocks + j
-            rows[pl.ds(start, count, stride=all_blocks), :] = tile[:, j * LANES : (j + 1) * LANES]
+            start = first * pitch + source * span_blocks + j
+            rows[pl.ds(start, count, stride=pitch), :] = tile[:, j * LANES : (j + 1) * LANES]
 
     loads[2].wait()
     mine = one_hot(tile)
@@ -133,18 +133,7 @@
         got = jnp.dot(mine, sig[:, c * piece : (c + 1) * piece], preferred_element_type=F32)
         for j in range(piece // LANES):
             start = me_t * span_blocks + c * (piece // LANES) + j
-            rows[pl.ds(start, slots, stride=all_blocks), :] = got[:, j * LANES : (j + 1) * LANES]
-
-    for d in range(1, n_t):
-        ask(d).wait_recv()
-        theirs = one_hot(wanted[d - 1])
-        for c in range(span // piece):
-            cut = slice(c * piece, (c + 1) * piece)
-            reply[d - 1, :, cut] = jnp.dot(
-                theirs, sig[:, cut], preferred_element_type=F32
-            ).astype(BF16)
-        for i in range(chunks):
-            send_rows(d, order(i)).start()
+            rows[pl.ds(start, slots, stride=pitch), :] = got[:, j * LANES : (j + 1) * LANES]
 
     loads[3].wait()
     waves = []
@@ -166,6 +155,17 @@
             preferred_element_type=F32,
         )
 
+    for d in range(1, n_t):
+        ask(d).wait_recv()
+        theirs = one_hot(wanted[d - 1])
+        for c in range(span // piece):
+            cut = slice(c * piece, (c + 1) * piece)
+            reply[d - 1, :, cut] = jnp.dot(
+                theirs, sig[:, cut], preferred_element_type=F32
+            ).astype(BF16)
+        for i in range(chunks):
+            send_rows(d, order(i)).start()
+
     lower = (iota((LANES, LANES), 0) >= iota((LANES, LANES), 1)).astype(F32).astype(BF16) > 0
 
     def circle(line):
@@ -214,7 +214,7 @@
             blocks = move // LANES
             rest = move - blocks * LANES
             turn = lax.rem(LANES - rest, LANES)
-            base = (k * n_slot + s) * all_blocks + blocks
+            base = (k * n_slot + s) * pitch + blocks
             turned = [
                 pltpu.roll(rows[pl.ds(base + j, out_blocks), :], turn, 1) for j in range(n_band + 1)
             ]
@@ -315,7 +315,7 @@
             pltpu.VMEM((n_t - 1, n_slot, LANES), jnp.int32),
             pltpu.VMEM((n_t - 1, slots, span), BF16),
             pltpu.VMEM((n_t - 1, slots, span), BF16),
-            pltpu.VMEM((slots * n_t * span // LANES, LANES), F32),
+            pltpu.VMEM((slots * (n_t * span // LANES + 1), LANES), F32),
             pltpu.VMEM((slots, (n_circ + 1) * LANES, LANES), BF16),
             pltpu.VMEM(((n_circ + 1) * LANES, LANES), BF16),
             pltpu.VMEM((slots, LANES), F32),

time: 21.3 us -> 21 us (0.986)
  Pallas kernels: 19.7 us -> 19.4 us
    pallas_call x1, Pallas kernels: 19.7 us -> 19.4 us  [shards(): pl.pallas_call(functools.partial(kernel, n_t, n_s), out_shape=jax.ShapeDt...]
where the time goes in v3:
time: 21 us; the launch traced here: 20.7 us
  Pallas kernels  19.4 us (92%)
  local copies, waits for them, and re-layouts  1.31 us (6%)
    pallas_call x1, Pallas kernels, shards(): pl.pallas_call(functools.partial(kernel, n_t, n_s), out_shape=jax.ShapeDt...  19.4 us
    unnamed x1, local copies, waits for them, and re-layouts  1.31 us

profile of v3, /device:TPU:0, one launch (start us, length us, event | category | flops | bytes accessed | tf_op | source)
XLA Modules:
  0.0 20.7 jit_solution(14837519429767114598)
XLA Ops:
  0.0 19.4 %shard_map.55 = f32[1,24,128]{2,1,0:T(8,128)} custom-call(s32[4,8]{1,0:T(4,128)} %bitcast.3, s32[8,4,8]{2,1,0:T(4,128)} %off_hbm.1, s32[8,4,8]{2,1,0:T(4,128)} %mov_hbm.1, bf16[8,4,8,300]{3,2,1,0:T(8,128)(2,1)} %wave_hbm.1, bf16[384,2048]{1,0:T(8,128)(2,1)} %sig_hbm.1), custom_call_target="tpu_custom_call" | custom-call | tf_op jit(solution)/shard_map/pallas_call | solution.py:302
  19.4 1.3 %copy.7 = f32[1,3072]{1,0:T(1,128)} copy(f32[1,3072]{1,0:T(1,128)} %bitcast.2) | data formatting | bytes 24576
